TPU v7x, 32 devices: a whole 2x2x4 slice. The times are simulated.
32 devices in a mesh: dp: 2 (over x), slab: 16 (over z, y, core).
Axes of the slice: x: 2, y: 2, z: 4, core: 2. Of those that a mesh axis runs over, the one named last changes fastest.
Arguments:
- field: float32 [2, 32, 128, 128, 128], P('dp', None, 'slab'), may hold values from -6 to 6
- cotangent: float32 [2, 32, 128, 128, 128], P('dp', None, 'slab'), may hold values from -6 to 6
- spec_weight: float32 [2, 32, 512, 1024], P(None, None, 'slab'), may hold values from -8 to 8
- bypass_weight: float32 [32, 32], replicated, may hold values from -1 to 1
Outputs:
- layer_out: float32 [2, 32, 128, 128, 128], P('dp', None, 'slab')
- grad_field: float32 [2, 32, 128, 128, 128], P('dp', None, 'slab')
- grad_spec: float32 [2, 32, 512, 1024], P(None, None, 'slab')
All inputs are finite; a program needn't handle non-finite values.
Results may differ from a plain program's by a relative error of at most 0.0001.
Values sent between devices are 32-bit elements; how exact they have to be, the bound alone decides.
No kernel may reach another device: no remote copies, remote signals or barrier semaphores. Data moves between devices by JAX's collectives and lax.ppermute only.
A program may use at most 384 MiB of HBM per device.

v0:
```python
import math
import jax
import jax.numpy as jnp
from jax import lax
from jax.sharding import PartitionSpec as P

GX = 128
GY = 128
GZ = 128
KX = 32
KY = 32
KZ = 16
precise = lax.Precision.HIGHEST


def wave_tables(length, count, signed):
    positions = jnp.arange(length, dtype=jnp.int32)
    indices = jnp.arange(count, dtype=jnp.int32)
    if signed:
        freqs = jnp.where(indices < count // 2, indices, indices - count)
    else:
        freqs = indices
    phase = positions[:, None] * freqs[None, :] % length
    angle = phase.astype(jnp.float32) * (2.0 * math.pi / length)
    return (jnp.cos(angle), jnp.sin(angle))


def gelu_exact(values):
    return jax.nn.gelu(values, approximate=False)


def plane_spectrum(data, weight, z_cos, z_sin, y_cos, y_sin):
    chans, planes = (data.shape[0], data.shape[1])
    part_re = jnp.einsum("cxyz,zk->cxky", data, z_cos, precision=precise)
    part_im = -jnp.einsum("cxyz,zk->cxky", data, z_sin, precision=precise)
    mid_re = jnp.einsum("cxky,yj->cxjk", part_re, y_cos, precision=precise) + jnp.einsum(
        "cxky,yj->cxjk", part_im, y_sin, precision=precise
    )
    mid_im = jnp.einsum("cxky,yj->cxjk", part_im, y_cos, precision=precise) - jnp.einsum(
        "cxky,yj->cxjk", part_re, y_sin, precision=precise
    )
    stacked = jnp.stack([mid_re * weight, mid_im * weight])
    return stacked.reshape(2, chans, planes, KY * KZ)


def along_first(moved, x_cos, x_sin):
    line_re, line_im = (moved[0], moved[1])
    full_re = jnp.einsum("cxp,xi->cpi", line_re, x_cos, precision=precise) + jnp.einsum(
        "cxp,xi->cpi", line_im, x_sin, precision=precise
    )
    full_im = jnp.einsum("cxp,xi->cpi", line_im, x_cos, precision=precise) - jnp.einsum(
        "cxp,xi->cpi", line_re, x_sin, precision=precise
    )
    return (full_re, full_im)


def back_first(spec_re, spec_im, x_cos, x_sin):
    wide_re = jnp.einsum("cpi,xi->cxp", spec_re, x_cos, precision=precise) - jnp.einsum(
        "cpi,xi->cxp", spec_im, x_sin, precision=precise
    )
    wide_im = jnp.einsum("cpi,xi->cxp", spec_re, x_sin, precision=precise) + jnp.einsum(
        "cpi,xi->cxp", spec_im, x_cos, precision=precise
    )
    return jnp.stack([wide_re, wide_im])


def plane_inverse(arrived, weight, z_cos, z_sin, y_cos, y_sin):
    chans, planes = (arrived.shape[1], arrived.shape[2])
    shaped = arrived.reshape(2, chans, planes, KY, KZ)
    wide_re, wide_im = (shaped[0], shaped[1])
    plane_re = jnp.einsum("cxjk,yj->cxky", wide_re, y_cos, precision=precise) - jnp.einsum(
        "cxjk,yj->cxky", wide_im, y_sin, precision=precise
    )
    plane_im = jnp.einsum("cxjk,yj->cxky", wide_re, y_sin, precision=precise) + jnp.einsum(
        "cxjk,yj->cxky", wide_im, y_cos, precision=precise
    )
    plane_re = plane_re * weight[:, None]
    plane_im = plane_im * weight[:, None]
    return jnp.einsum("cxky,zk->cxyz", plane_re, z_cos, precision=precise) - jnp.einsum(
        "cxky,zk->cxyz", plane_im, z_sin, precision=precise
    )


def on_device(field, cotangent, spec_weight, bypass_weight):
    count = lax.axis_size("slab")
    pairs = KY * KZ // count
    chans = field.shape[1]
    z_cos, z_sin = wave_tables(GZ, KZ, False)
    y_cos, y_sin = wave_tables(GY, KY, True)
    x_cos, x_sin = wave_tables(GX, KX, True)
    kz_index = jnp.arange(KZ, dtype=jnp.int32)
    fold = jnp.where(kz_index == 0, 1.0, 2.0).astype(jnp.float32) / float(GX * GY * GZ)
    ones = jnp.ones((KZ,), jnp.float32)
    weights = spec_weight.reshape(2, chans, pairs, KX, chans)
    w_real = weights[0]
    w_imag = weights[1]
    source = field[0]
    local_spec = plane_spectrum(source, ones, z_cos, z_sin, y_cos, y_sin)
    moved = lax.all_to_all(local_spec, "slab", split_axis=3, concat_axis=2, tiled=True)
    hat_re, hat_im = along_first(moved, x_cos, x_sin)
    mix_re = jnp.einsum("cpi,cpio->opi", hat_re, w_real, precision=precise) - jnp.einsum(
        "cpi,cpio->opi", hat_im, w_imag, precision=precise
    )
    mix_im = jnp.einsum("cpi,cpio->opi", hat_re, w_imag, precision=precise) + jnp.einsum(
        "cpi,cpio->opi", hat_im, w_real, precision=precise
    )
    outgoing = back_first(mix_re, mix_im, x_cos, x_sin)
    arrived = lax.all_to_all(outgoing, "slab", split_axis=2, concat_axis=3, tiled=True)
    spectral = plane_inverse(arrived, fold, z_cos, z_sin, y_cos, y_sin)
    pre = spectral + jnp.einsum("co,cxyz->oxyz", bypass_weight, source, precision=precise)
    result, pullback = jax.vjp(gelu_exact, pre)
    grad_pre = pullback(cotangent[0])[0]
    fold_grid = jnp.broadcast_to(fold, (KY, KZ))
    cot_spec = plane_spectrum(grad_pre, fold_grid, z_cos, z_sin, y_cos, y_sin)
    cot_moved = lax.all_to_all(cot_spec, "slab", split_axis=3, concat_axis=2, tiled=True)
    grad_re, grad_im = along_first(cot_moved, x_cos, x_sin)
    own_real = jnp.einsum("cpi,opi->cpio", hat_re, grad_re, precision=precise) + jnp.einsum(
        "cpi,opi->cpio", hat_im, grad_im, precision=precise
    )
    own_imag = jnp.einsum("cpi,opi->cpio", hat_re, grad_im, precision=precise) - jnp.einsum(
        "cpi,opi->cpio", hat_im, grad_re, precision=precise
    )
    summed = lax.psum(jnp.stack([own_real, own_imag]), "dp")
    grad_spec = summed.reshape(2, chans, pairs, KX * chans)
    input_re = jnp.einsum("opi,cpio->cpi", grad_re, w_real, precision=precise) + jnp.einsum(
        "opi,cpio->cpi", grad_im, w_imag, precision=precise
    )
    input_im = jnp.einsum("opi,cpio->cpi", grad_im, w_real, precision=precise) - jnp.einsum(
        "opi,cpio->cpi", grad_re, w_imag, precision=precise
    )
    grad_out = back_first(input_re, input_im, x_cos, x_sin)
    grad_arrived = lax.all_to_all(grad_out, "slab", split_axis=2, concat_axis=3, tiled=True)
    back_field = plane_inverse(grad_arrived, ones, z_cos, z_sin, y_cos, y_sin)
    back_field = back_field + jnp.einsum(
        "co,oxyz->cxyz", bypass_weight, grad_pre, precision=precise
    )
    return (result[None], back_field[None], grad_spec)


def solution(mesh):
    in_specs = (
        P("dp", None, "slab", None, None),
        P("dp", None, "slab", None, None),
        P(None, None, "slab", None),
        P(),
    )
    out_specs = (
        P("dp", None, "slab", None, None),
        P("dp", None, "slab", None, None),
        P(None, None, "slab", None),
    )
    return jax.shard_map(
        on_device, mesh=mesh, in_specs=in_specs, out_specs=out_specs, check_vma=False
    )
```

profile of v0, /device:TPU:0, one launch (start us, length us, event | category | flops | bytes accessed | tf_op | source)
XLA Modules:
  0.0 795.2 jit_solution(8337754750162333702)
XLA Ops:
  7.2 17.2 %convolution_bitcast_fusion.1 = f32[32,8,16,128]{3,2,1,0:T(8,128)S(1)} fusion(f32[1,32,8,128,128]{4,3,2,1,0:T(8,128)} %param.4), kind=kOutput, calls=%fused_computation.101 | convolution fusion | flops 805335040 | bytes 18874368 | tf_op jit(solution)/shard_map/cxyz,zk->cxky/dot_general | solution.py:34
  24.4 14.7 %negate_bitcast_fusion.1 = f32[32,8,16,128]{3,2,1,0:T(8,128)S(1)} fusion(f32[1,32,8,128,128]{4,3,2,1,0:T(8,128)S(1)} %copy-done.2), kind=kOutput, calls=%fused_computation.75 | convolution fusion | flops 805859328 | bytes 18874368 | tf_op jit(solution)/shard_map/cxyz,zk->cxky/dot_general | solution.py:35
  39.1 9.8 %fusion.57 = f32[32,32,8,16]{1,0,3,2:T(8,128)S(1)} fusion(f32[32,8,16,128]{3,2,1,0:T(8,128)S(1)} %negate_bitcast_fusion.1, s32[32]{0:T(128)S(1)} %compare_select_fusion), kind=kOutput, calls=%fused_computation.92 | convolution fusion | flops 201383936 | bytes 2621568 | tf_op jit(solution)/shard_map/cxky,yj->cxjk/dot_general | solution.py:39
  48.9 9.7 %fusion.59 = f32[32,32,8,16]{1,0,3,2:T(8,128)S(1)} fusion(f32[32,8,16,128]{3,2,1,0:T(8,128)S(1)} %negate_bitcast_fusion.1, s32[32]{0:T(128)S(1)} %compare_select_fusion), kind=kOutput, calls=%fused_computation.94 | convolution fusion | flops 201383936 | bytes 2621568 | tf_op jit(solution)/shard_map/cxky,yj->cxjk/dot_general | solution.py:36
  58.7 10.2 %add_bitcast_fusion.1 = f32[32,8,32,16]{0,2,3,1:T(8,128)S(1)} fusion(f32[32,32,8,16]{1,0,3,2:T(8,128)S(1)} %fusion.59, f32[32,8,16,128]{3,2,1,0:T(8,128)S(1)} %convolution_bitcast_fusion.1, s32[32]{0:T(128)S(1)} %compare_select_fusion), kind=kOutput, calls=%fused_computation.74 | convolution fusion | flops 201515008 | bytes 3145856 | tf_op jit(solution)/shard_map/cxky,yj->cxjk/dot_general | solution.py:36
  68.8 9.8 %subtract_bitcast_fusion.1 = f32[32,8,32,16]{0,2,3,1:T(8,128)S(1)} fusion(f32[32,32,8,16]{1,0,3,2:T(8,128)S(1)} %fusion.57, f32[32,8,16,128]{3,2,1,0:T(8,128)S(1)} %convolution_bitcast_fusion.1, s32[32]{0:T(128)S(1)} %compare_select_fusion), kind=kOutput, calls=%fused_computation.73 | convolution fusion | flops 201515008 | bytes 3145856 | tf_op jit(solution)/shard_map/cxky,yj->cxjk/dot_general | solution.py:39
  90.8 7.4 all-to-all-start
  98.2 8.5 %fusion.393 = (f32[1,32,32,1024]{3,2,1,0:T(8,128)}, f32[1,32,32,1024]{3,2,1,0:T(8,128)}) fusion(f32[2,32,32,1024]{3,2,1,0:T(8,128)} %param.6), kind=kLoop, calls=%fused_computation.379 | loop fusion | bytes 16777216 | tf_op jit(solution)/shard_map/slice | solution.py:95
  106.7 11.6 %squeeze.39 = f32[32,32,32,32]{3,2,1,0:T(8,128)} reshape(f32[1,32,32,1024]{3,2,1,0:T(8,128)} %get-tuple-element.17) | data formatting | bytes 8388608 | tf_op jit(solution)/shard_map/squeeze | solution.py:95
  118.3 11.6 %squeeze.40 = f32[32,32,32,32]{3,2,1,0:T(8,128)} reshape(f32[1,32,32,1024]{3,2,1,0:T(8,128)} %get-tuple-element.18) | data formatting | bytes 8388608 | tf_op jit(solution)/shard_map/squeeze | solution.py:96
  136.5 6.6 copy.241
  160.0 12.7 %multiply_reduce_fusion.5 = (f32[32,32,32]{2,1,0:T(8,128)S(1)}, f32[32,32,32]{2,1,0:T(8,128)S(1)}, f32[32,32,32]{2,1,0:T(8,128)S(1)}, f32[32,32,32]{2,1,0:T(8,128)S(1)}) fusion(f32[32,32,32,32]{3,2,1,0:T(8,128)} %squeeze.40, f32[32,32,32]{1,0,2:T(8,128)S(1)} %fusion.76, f32[32,32,32]{1,0,2:T(8,128)S(1)} %fusion.82, f32[32,32,32,32]{3,2,1,0:T(8,128)} %squeeze.39), kind=kLoop, calls=%fused_computation.18 | loop fusion | flops 8257536 | bytes 9175040
  192.7 30.5 %fusion.10 = f32[32,8,128,128]{3,0,2,1:T(8,128)} fusion(f32[32,8,128,128]{3,2,1,0:T(8,128)} %bitcast.317, f32[32,32]{1,0:T(8,128)S(1)} %copy-done), kind=kOutput, calls=%fused_computation.24 | convolution fusion | flops 1610612736 | bytes 33558528 | tf_op jit(solution)/shard_map/co,cxyz->oxyz/dot_general | solution.py:110
  258.3 29.0 %fusion.38 = f32[32,8,128,128]{3,2,1,0:T(8,128)} fusion(f32[32,8,16,128]{3,2,1,0:T(8,128)S(1)} %fusion.156, f32[32,8,16,128]{3,2,1,0:T(8,128)S(1)} %copy-done.4, f32[16]{0:T(128)S(1)} %fusion.229), kind=kOutput, calls=%fused_computation.70 | convolution fusion | flops 806383616 | bytes 20971584 | tf_op jit(solution)/shard_map/cxky,zk->cxyz/dot_general | solution.py:79
  287.3 69.5 %fusion.6 = (f32[32,8,128,128]{3,2,1,0:T(8,128)S(1)}, f32[32,8,128,128]{3,2,1,0:T(8,128)}, f32[32,8,128,128]{3,2,1,0:T(8,128)}) fusion(f32[1,32,8,128,128]{4,3,2,1,0:T(8,128)} %param.5, f32[32,8,128,128]{3,0,2,1:T(8,128)} %fusion.10, f32[32,8,128,128]{3,2,1,0:T(8,128)} %fusion.38, f32[32,8,16,128]{3,2,1,0:T(8,128)S(1)} %fusion.142, ...), kind=kOutput, calls=%fused_computation.11 | convolution fusion | flops 1112567808 | bytes 104857664 | tf_op jit(solution)/shard_map/cxky,zk->cxyz/dot_general | solution.py:79
  356.9 14.6 %negate_bitcast_fusion = f32[32,8,16,128]{3,2,1,0:T(8,128)S(1)} fusion(f32[32,8,128,128]{3,2,1,0:T(8,128)S(1)} %get-tuple-element.15), kind=kOutput, calls=%fused_computation.67 | convolution fusion | flops 805859328 | bytes 18874368 | tf_op jit(solution)/shard_map/cxyz,zk->cxky/dot_general | solution.py:35
  371.4 14.8 %convolution_bitcast_fusion = f32[32,8,16,128]{3,2,1,0:T(8,128)S(1)} fusion(f32[32,8,128,128]{3,2,1,0:T(8,128)S(1)} %get-tuple-element.15), kind=kOutput, calls=%fused_computation.100 | convolution fusion | flops 805335040 | bytes 18874368 | tf_op jit(solution)/shard_map/cxyz,zk->cxky/dot_general | solution.py:34
  386.2 9.8 %fusion.45 = f32[32,32,8,16]{1,0,3,2:T(8,128)S(1)} fusion(f32[32,8,16,128]{3,2,1,0:T(8,128)S(1)} %negate_bitcast_fusion, s32[32]{0:T(128)S(1)} %copy-done.11), kind=kOutput, calls=%fused_computation.80 | convolution fusion | flops 201383936 | bytes 2621568 | tf_op jit(solution)/shard_map/cxky,yj->cxjk/dot_general | solution.py:39
  396.0 9.8 %fusion.47 = f32[32,32,8,16]{1,0,3,2:T(8,128)S(1)} fusion(f32[32,8,16,128]{3,2,1,0:T(8,128)S(1)} %negate_bitcast_fusion, s32[32]{0:T(128)S(1)} %copy-done.11), kind=kOutput, calls=%fused_computation.82 | convolution fusion | flops 201383936 | bytes 2621568 | tf_op jit(solution)/shard_map/cxky,yj->cxjk/dot_general | solution.py:36
  405.8 10.2 %multiply_bitcast_fusion.2 = f32[32,8,32,16]{0,2,3,1:T(8,128)S(1)} fusion(f32[32,32,8,16]{1,0,3,2:T(8,128)S(1)} %fusion.47, f32[32,8,16,128]{3,2,1,0:T(8,128)S(1)} %convolution_bitcast_fusion, f32[16]{0:T(128)S(1)} %fusion.229, s32[32]{0:T(128)S(1)} %copy-done.11), kind=kOutput, calls=%fused_computation.66 | convolution fusion | flops 201646080 | bytes 3145920 | tf_op jit(solution)/shard_map/cxky,yj->cxjk/dot_general | solution.py:36
  416.0 9.8 %multiply_bitcast_fusion.1 = f32[32,8,32,16]{0,2,3,1:T(8,128)S(1)} fusion(f32[32,32,8,16]{1,0,3,2:T(8,128)S(1)} %fusion.45, f32[32,8,16,128]{3,2,1,0:T(8,128)S(1)} %convolution_bitcast_fusion, f32[16]{0:T(128)S(1)} %fusion.229, s32[32]{0:T(128)S(1)} %copy-done.11), kind=kOutput, calls=%fused_computation.65 | convolution fusion | flops 201646080 | bytes 3145920 | tf_op jit(solution)/shard_map/cxky,yj->cxjk/dot_general | solution.py:39
  437.1 30.6 %all_to_all.60 = f32[16,1,16384]{2,1,0:T(1,128)S(1)} all-to-all(f32[16,1,16384]{2,1,0:T(1,128)S(1)} %reshape.87), channel_id=1, replica_groups=mesh['dp'=2,'slab'=16] {'slab'}, dimensions={0} | all-to-all | bytes 2097152 | tf_op jit(solution)/shard_map/all_to_all | solution.py:115
  473.7 6.8 copy.243
  499.7 31.3 %add_bitcast_fusion = (f32[1,32,32,32,32]{4,3,2,1,0:T(8,128)}, f32[1,32,32,32,32]{4,3,2,1,0:T(8,128)}, f32[32,32,32]{1,0,2:T(8,128)S(1)}, f32[32,32,32]{1,0,2:T(...) fusion(f32[32,32,32]{2,1,0:T(8,128)} %copy.247, f32[32,32,32]{2,1,0:T(8,128)} %copy.246, ...), kind=kLoop, calls=%fused_computation.27 | loop fusion | flops 14548992 | bytes 17825792 | tf_op jit(solution)/shard_map/stack | solution.py:123
  531.0 24.1 %pad_maximum_fusion = f32[2,32,32,32,32]{4,3,2,1,0:T(8,128)} fusion(f32[1,32,32,32,32]{4,3,2,1,0:T(8,128)} %get-tuple-element.28, f32[1,32,32,32,32]{4,3,2,1,0:T(8,128)} %get-tuple-element.27), kind=kLoop, calls=%fused_computation | loop fusion | flops 2097152 | bytes 16777216 | tf_op jit(solution)/shard_map/stack | solution.py:123
  555.1 26.1 %reshape.58 = f32[2,32,32,1024]{3,2,1,0:T(8,128)} reshape(f32[2,32,32,32,32]{4,3,2,1,0:T(8,128)} %pad_maximum_fusion) | data formatting | bytes 16777216 | tf_op jit(solution)/shard_map/reshape | solution.py:124
  581.2 33.5 %fusion.8 = f32[8,128,128,32]{2,3,1,0:T(8,128)} fusion(f32[32,8,128,128]{3,2,1,0:T(8,128)} %copy-done.1, f32[32,32]{1,0:T(8,128)S(1)} %copy-done), kind=kOutput, calls=%fused_computation.21 | convolution fusion | flops 1610612736 | bytes 33558528 | tf_op jit(solution)/shard_map/co,oxyz->cxyz/dot_general | solution.py:134
  631.8 19.1 %multiply_bitcast_fusion = f32[1,32,8,128,128]{4,3,2,1,0:T(8,128)} fusion(f32[32,8,128,128]{3,2,1,0:T(8,128)} %get-tuple-element.16, f32[32,8,128,128]{3,2,1,0:T(8,128)} %get-tuple-element.33), kind=kLoop, calls=%fused_computation.28 | loop fusion | flops 8388608 | bytes 50331648 | tf_op jit(solution)/shard_map/broadcast_in_dim | solution.py:137
  687.7 28.8 %fusion.34 = f32[32,8,128,128]{3,2,1,0:T(8,128)} fusion(f32[32,8,16,128]{3,2,1,0:T(8,128)S(1)} %fusion.150, f32[32,8,16,128]{3,2,1,0:T(8,128)S(1)} %fusion.138), kind=kOutput, calls=%fused_computation.63 | convolution fusion | flops 805859328 | bytes 20971520 | tf_op jit(solution)/shard_map/cxky,zk->cxyz/dot_general | solution.py:79
  716.6 45.4 %fusion.1 = f32[1,32,8,128,128]{4,3,2,1,0:T(8,128)} fusion(f32[8,128,128,32]{2,3,1,0:T(8,128)S(1)} %bitcast.319, f32[32,8,128,128]{3,2,1,0:T(8,128)} %fusion.34, f32[32,8,16,128]{3,2,1,0:T(8,128)S(1)} %fusion.136, f32[32,8,16,128]{3,2,1,0:T(8,128)S(1)} %fusion.148), kind=kOutput, calls=%fused_computation.4 | convolution fusion | flops 814247936 | bytes 54525952 | tf_op jit(solution)/shard_map/cxky,zk->cxyz/dot_general | solution.py:79
  762.0 17.6 %all-reduce.2.cloned.1.call-done = f32[2,32,32,1024]{3,2,1,0:T(8,128)} async-done(((f32[2,32,32,1024]{3,2,1,0:T(8,128)}), f32[2,32,32,1024]{3,2,1,0:T(8,128)}) %all-reduce.2.cloned.1.call-update) | async-done | bytes 8388624 | tf_op jit(solution)/shard_map/psum | solution.py:123
  779.6 8.4 %copy.337 = f32[2,32,32,1024]{3,2,1,0:T(8,128)} copy(f32[2,32,32,1024]{3,2,1,0:T(8,128)} %all-reduce.2.cloned.1.call-done) | data formatting | bytes 16777216
  (111 shorter events, 180.6 us)
Async XLA Ops:
  7.2 185.6 %copy-start = (f32[32,32]{1,0:T(8,128)S(1)}, f32[32,32]{1,0:T(8,128)}, u32[]{:S(2)}) copy-start(f32[32,32]{1,0:T(8,128)} %param.7) | copy-start | bytes 12292
  7.2 249.1 %copy-start.10 = (s32[32]{0:T(128)}, s32[32]{0:T(128)S(1)}, u32[]{:S(2)}) copy-start(s32[32]{0:T(128)S(1)} %compare_select_fusion) | copy-start | bytes 388
  7.2 17.2 %copy-start.2 = (f32[1,32,8,128,128]{4,3,2,1,0:T(8,128)S(1)}, f32[1,32,8,128,128]{4,3,2,1,0:T(8,128)}, u32[]{:S(2)}) copy-start(f32[1,32,8,128,128]{4,3,2,1,0:T(8,128)} %param.4) | copy-start | bytes 50331652
  90.8 39.2 %all-to-all-start = ((f32[16,1,16384]{2,1,0:T(1,128)}), f32[16,1,16384]{2,1,0:T(1,128)S(1)}, u32[]{:S(2)}, u32[]{:S(2)}) async-start(f32[16,1,16384]{2,1,0:T(1,128)} %reshape.83), calls=%async_computation | async-start | bytes 2097152 | tf_op jit(solution)/shard_map/all_to_all | solution.py:99
  156.4 16.3 %copy-start.5 = (f32[32,32,32]{1,0,2:T(8,128)}, f32[32,32,32]{1,0,2:T(8,128)S(1)}, u32[]{:S(2)}) copy-start(f32[32,32,32]{1,0,2:T(8,128)S(1)} %fusion.76) | copy-start | bytes 393220
  160.0 12.7 %copy-start.7 = (f32[32,32,32]{1,0,2:T(8,128)}, f32[32,32,32]{1,0,2:T(8,128)S(1)}, u32[]{:S(2)}) copy-start(f32[32,32,32]{1,0,2:T(8,128)S(1)} %fusion.82) | copy-start | bytes 393220
  186.7 36.6 %all-to-all-start.1 = ((f32[16,1,16384]{2,1,0:T(1,128)}), f32[16,1,16384]{2,1,0:T(1,128)S(1)}, u32[]{:S(2)}, u32[]{:S(2)}) async-start(f32[16,1,16384]{2,1,0:T(1,128)} %reshape.85), calls=%async_computation.1 | async-start | bytes 2097152 | tf_op jit(solution)/shard_map/all_to_all | solution.py:108
  192.7 587.0 %all-reduce.2.cloned.1.call-start = ((), (), s32[]{:S(2)}) async-start(), calls=%async_computation.4 | async-start | bytes 16777216 | tf_op jit(solution)/shard_map/psum | solution.py:123
  254.3 4.0 copy-start.4
  258.3 29.1 %copy-start.9 = (f32[32,8,16,128]{3,2,1,0:T(8,128)S(1)}, f32[32,8,16,128]{3,2,1,0:T(8,128)}, u32[]{:S(2)}) copy-start(f32[32,8,16,128]{3,2,1,0:T(8,128)} %fusion.154) | copy-start | bytes 6291460
  356.9 14.6 %copy-start.1 = (f32[32,8,128,128]{3,2,1,0:T(8,128)}, f32[32,8,128,128]{3,2,1,0:T(8,128)S(1)}, u32[]{:S(2)}) copy-start(f32[32,8,128,128]{3,2,1,0:T(8,128)S(1)} %get-tuple-element.15) | copy-start | bytes 50331652
  371.4 14.8 %copy-start.11 = (s32[32]{0:T(128)S(1)}, s32[32]{0:T(128)}, u32[]{:S(2)}) copy-start(s32[32]{0:T(128)} %copy-done.10) | copy-start | bytes 388
  490.3 9.5 %copy-start.6 = (f32[32,32,32]{1,0,2:T(8,128)S(1)}, f32[32,32,32]{1,0,2:T(8,128)}, u32[]{:S(2)}) copy-start(f32[32,32,32]{1,0,2:T(8,128)} %copy-done.5) | copy-start | bytes 393220
  490.3 9.4 %copy-start.8 = (f32[32,32,32]{1,0,2:T(8,128)S(1)}, f32[32,32,32]{1,0,2:T(8,128)}, u32[]{:S(2)}) copy-start(f32[32,32,32]{1,0,2:T(8,128)} %copy-done.7) | copy-start | bytes 393220
  626.8 28.0 %all-to-all-start.3 = ((f32[16,1,16384]{2,1,0:T(1,128)}), f32[16,1,16384]{2,1,0:T(1,128)S(1)}, u32[]{:S(2)}, u32[]{:S(2)}) async-start(f32[16,1,16384]{2,1,0:T(1,128)} %reshape.89), calls=%async_computation.3 | async-start | bytes 2097152 | tf_op jit(solution)/shard_map/all_to_all | solution.py:132
  679.7 4.0 copy-start.3
  685.7 30.9 %slice-start = ((s8[16777216]{0:T(1024)(128)(4,1)}), s8[4194304]{0:T(1024)(128)(4,1)S(1)}, s32[]{:S(2)}) async-start(s8[16777216]{0:T(1024)(128)(4,1)} %bitcast.318), calls=%async_computation.5 | async-start | bytes 8388608
  687.7 28.9 %slice-start.1 = ((s8[16777216]{0:T(1024)(128)(4,1)}), s8[4194304]{0:T(1024)(128)(4,1)S(1)}, s32[]{:S(2)}) async-start(s8[16777216]{0:T(1024)(128)(4,1)} %bitcast.318), calls=%async_computation.6 | async-start | bytes 8388608
  687.7 28.9 %slice-start.2 = ((s8[16777216]{0:T(1024)(128)(4,1)}), s8[4194304]{0:T(1024)(128)(4,1)S(1)}, s32[]{:S(2)}) async-start(s8[16777216]{0:T(1024)(128)(4,1)} %bitcast.318), calls=%async_computation.7 | async-start | bytes 8388608
  687.7 28.9 %slice-start.3 = ((s8[16777216]{0:T(1024)(128)(4,1)}), s8[4194304]{0:T(1024)(128)(4,1)S(1)}, s32[]{:S(2)}) async-start(s8[16777216]{0:T(1024)(128)(4,1)} %bitcast.318), calls=%async_computation.8 | async-start | bytes 8388608
Sparse Core Ops, SparseCore 0:
  581.3 198.3 all-reduce.1
where the time goes:
time: 802 us; the launch traced here: 795 us
  matrix products  430 us (54%)
  local copies, waits for them, and re-layouts  179 us (22%)
  other arithmetic  101 us (13%)
  blocking collectives  30.6 us (4%)
  waiting for transfers between devices  21.5 us (3%)
  starting transfers between devices  18.5 us (2%)
  between operations  15 us (2%)
    dot_general x2, matrix products, plane_inverse(): jnp.einsum('cxky,zk->cxyz', plane_im, z_sin, precision=precise)  115 us
    dot_general x2, matrix products, plane_inverse(): jnp.einsum('cxky,zk->cxyz', plane_re, z_cos, precision=precise)  57.9 us
    another operation x2, other arithmetic, on_device(): summed = lax.psum(jnp.stack([own_real, own_imag]), 'dp')  55.3 us
    unnamed x43, local copies, waits for them, and re-layouts  39.9 us
    dot_general x1, matrix products, on_device(): jnp.einsum('co,oxyz->cxyz', bypass_weight, grad_pre, precision=precise)  33.5 us
    dot_general x2, matrix products, plane_spectrum(): part_re = jnp.einsum('cxyz,zk->cxky', data, z_cos, precision=precise)  31.9 us
    all_to_all x1, blocking collectives, on_device(): lax.all_to_all(cot_spec, 'slab', split_axis=3, concat_axis=2, tiled=True)  30.6 us
    dot_general x1, matrix products, on_device(): jnp.einsum('co,cxyz->oxyz', bypass_weight, source, precision=precise)  30.5 us
  transfers between devices with their start and end apart: 4, of which 2 were waited for; matrix products, arithmetic and copies ran while one was open for 29% of the time, Pallas kernels for 0%

commit v1 on v0

--- a/solution.py
+++ b/solution.py
@@ -120,7 +120,7 @@
     own_imag = jnp.einsum("cpi,opi->cpio", hat_re, grad_im, precision=precise) - jnp.einsum(
         "cpi,opi->cpio", hat_im, grad_re, precision=precise
     )
-    summed = lax.psum(jnp.stack([own_real, own_imag]), "dp")
+    summed = jnp.sum(lax.all_gather(jnp.stack([own_real, own_imag]), "dp"), axis=0)
     grad_spec = summed.reshape(2, chans, pairs, KX * chans)
     input_re = jnp.einsum("opi,cpio->cpi", grad_re, w_real, precision=precise) + jnp.einsum(
         "opi,cpio->cpi", grad_im, w_imag, precision=precise

time: 802 us -> 1400 us (1.75)
  waiting for transfers between devices: 21.5 us -> 585 us
  other arithmetic: 101 us -> 137 us
    all_gather x0 -> x1, waiting for transfers between devices: none -> 583 us  [on_device(): lax.all_gather(jnp.stack([own_real, own_imag]), 'dp')]
    reduce_sum x0 -> x1, other arithmetic: none -> 34.3 us  [on_device(): jnp.sum(lax.all_gather(jnp.stack([own_real, own_imag]), 'dp'), axis=0)]
    psum x1 -> x0, waiting for transfers between devices: 17.6 us -> none  [on_device(): summed = lax.psum(jnp.stack([own_real, own_imag]), 'dp')]
    unnamed x43 -> x42, local copies, waits for them, and re-layouts: 39.9 us -> 33.9 us
  transfers between devices with their start and end apart: 4 -> 4, of which waited for: 2 -> 2; matrix products, arithmetic and copies ran while one was open for 29% -> 17% of each run, Pallas kernels for 0% -> 0%
where the time goes in v1:
time: 1400 us
  waiting for transfers between devices  585 us (42%)
  matrix products  437 us (31%)
  local copies, waits for them, and re-layouts  173 us (12%)
  other arithmetic  137 us (10%)
  blocking collectives  30.7 us (2%)
  starting transfers between devices  18.5 us (1%)
  between operations  15.2 us (1%)
    all_gather x1, waiting for transfers between devices, on_device(): lax.all_gather(jnp.stack([own_real, own_imag]), 'dp')  583 us
    dot_general x2, matrix products, plane_inverse(): jnp.einsum('cxky,zk->cxyz', plane_im, z_sin, precision=precise)  115 us
    dot_general x2, matrix products, plane_inverse(): jnp.einsum('cxky,zk->cxyz', plane_re, z_cos, precision=precise)  58.1 us
    another operation x2, other arithmetic, on_device(): jnp.stack([own_real, own_imag])  55.5 us
    dot_general x1, matrix products, on_device(): jnp.einsum('co,oxyz->cxyz', bypass_weight, grad_pre, precision=precise)  36.7 us
    reduce_sum x1, other arithmetic, on_device(): jnp.sum(lax.all_gather(jnp.stack([own_real, own_imag]), 'dp'), axis=0)  34.3 us
    unnamed x42, local copies, waits for them, and re-layouts  33.9 us
    dot_general x2, matrix products, plane_spectrum(): part_im = -jnp.einsum('cxyz,zk->cxky', data, z_sin, precision=precise)  31.8 us
  transfers between devices with their start and end apart: 4, of which 2 were waited for; matrix products, arithmetic and copies ran while one was open for 17% of the time, Pallas kernels for 0%

profile of v1, /device:TPU:0, one launch (start us, length us, event | category | flops | bytes accessed | tf_op | source)
XLA Modules:
  0.0 1396.6 jit_solution(18258210766896265682)
XLA Ops:
  7.2 17.2 %negate_bitcast_fusion.1 = f32[32,8,16,128]{3,2,1,0:T(8,128)S(1)} fusion(f32[1,32,8,128,128]{4,3,2,1,0:T(8,128)} %param.4), kind=kOutput, calls=%fused_computation.75 | convolution fusion | flops 805859328 | bytes 18874368 | tf_op jit(solution)/shard_map/cxyz,zk->cxky/dot_general | solution.py:35
  24.5 14.8 %convolution_bitcast_fusion.1 = f32[32,8,16,128]{3,2,1,0:T(8,128)S(1)} fusion(f32[1,32,8,128,128]{4,3,2,1,0:T(8,128)S(1)} %copy-done.2), kind=kOutput, calls=%fused_computation.101 | convolution fusion | flops 805335040 | bytes 18874368 | tf_op jit(solution)/shard_map/cxyz,zk->cxky/dot_general | solution.py:34
  39.3 9.8 fusion.57
  49.0 9.7 fusion.59
  58.8 10.2 subtract_bitcast_fusion.1
  70.2 9.9 add_bitcast_fusion.1
  90.9 7.4 all-to-all-start
  98.3 8.5 fusion.393
  106.9 11.6 squeeze.40
  118.5 11.7 squeeze.39
  136.5 6.6 copy.245
  160.1 12.7 multiply_reduce_fusion.5
  192.8 30.5 %fusion.10 = f32[32,8,128,128]{3,0,2,1:T(8,128)} fusion(f32[32,8,128,128]{3,2,1,0:T(8,128)} %bitcast.318, f32[32,32]{1,0:T(8,128)S(1)} %copy-done), kind=kOutput, calls=%fused_computation.24 | convolution fusion | flops 1610612736 | bytes 33558528 | tf_op jit(solution)/shard_map/co,cxyz->oxyz/dot_general | solution.py:110
  258.3 29.0 %fusion.38 = f32[32,8,128,128]{3,2,1,0:T(8,128)} fusion(f32[32,8,16,128]{3,2,1,0:T(8,128)S(1)} %copy-done.4, f32[32,8,16,128]{3,2,1,0:T(8,128)S(1)} %fusion.144, f32[16]{0:T(128)S(1)} %fusion.229), kind=kOutput, calls=%fused_computation.70 | convolution fusion | flops 806383616 | bytes 20971584 | tf_op jit(solution)/shard_map/cxky,zk->cxyz/dot_general | solution.py:79
  287.3 69.5 %fusion.6 = (f32[32,8,128,128]{3,2,1,0:T(8,128)S(1)}, f32[32,8,128,128]{3,2,1,0:T(8,128)}, f32[32,8,128,128]{3,2,1,0:T(8,128)}) fusion(f32[1,32,8,128,128]{4,3,2,1,0:T(8,128)} %param.5, f32[32,8,128,128]{3,0,2,1:T(8,128)} %fusion.10, f32[32,8,128,128]{3,2,1,0:T(8,128)} %fusion.38, f32[32,8,16,128]{3,2,1,0:T(8,128)S(1)} %copy-done.9, ...), kind=kOutput, calls=%fused_computation.11 | convolution fusion | flops 1112567808 | bytes 104857664 | tf_op jit(solution)/shard_map/cxky,zk->cxyz/dot_general | solution.py:79
  356.8 14.6 %negate_bitcast_fusion = f32[32,8,16,128]{3,2,1,0:T(8,128)S(1)} fusion(f32[32,8,128,128]{3,2,1,0:T(8,128)S(1)} %get-tuple-element.15), kind=kOutput, calls=%fused_computation.67 | convolution fusion | flops 805859328 | bytes 18874368 | tf_op jit(solution)/shard_map/cxyz,zk->cxky/dot_general | solution.py:35
  371.4 14.8 %convolution_bitcast_fusion = f32[32,8,16,128]{3,2,1,0:T(8,128)S(1)} fusion(f32[32,8,128,128]{3,2,1,0:T(8,128)S(1)} %get-tuple-element.15), kind=kOutput, calls=%fused_computation.100 | convolution fusion | flops 805335040 | bytes 18874368 | tf_op jit(solution)/shard_map/cxyz,zk->cxky/dot_general | solution.py:34
  386.2 9.8 fusion.45
  396.0 9.7 fusion.47
  405.7 10.2 multiply_bitcast_fusion.1
  417.2 9.9 multiply_bitcast_fusion.2
  437.0 30.7 %all_to_all.60 = f32[16,1,16384]{2,1,0:T(1,128)S(1)} all-to-all(f32[16,1,16384]{2,1,0:T(1,128)S(1)} %reshape.88), channel_id=1, replica_groups=mesh['dp'=2,'slab'=16] {'slab'}, dimensions={0} | all-to-all | bytes 2097152 | tf_op jit(solution)/shard_map/all_to_all | solution.py:115
  473.5 6.8 copy.247
  505.0 31.3 %add_bitcast_fusion = (f32[1,32,32,32,32]{4,3,2,1,0:T(8,128)}, f32[1,32,32,32,32]{4,3,2,1,0:T(8,128)}, f32[32,32,32]{1,0,2:T(8,128)S(1)}, f32[32,32,32]{1,0,2:T(...) fusion(f32[32,32,32]{2,1,0:T(8,128)} %copy.251, f32[32,32,32]{2,1,0:T(8,128)} %copy.250, ...), kind=kLoop, calls=%fused_computation.27 | loop fusion | flops 14548992 | bytes 17825792 | tf_op jit(solution)/shard_map/stack | solution.py:123
  536.2 24.2 %pad_maximum_fusion = f32[2,32,32,32,32]{4,3,2,1,0:T(8,128)} fusion(f32[1,32,32,32,32]{4,3,2,1,0:T(8,128)} %get-tuple-element.28, f32[1,32,32,32,32]{4,3,2,1,0:T(8,128)} %get-tuple-element.27), kind=kLoop, calls=%fused_computation | loop fusion | flops 2097152 | bytes 16777216 | tf_op jit(solution)/shard_map/stack | solution.py:123
  560.5 36.7 %fusion.8 = f32[8,128,128,32]{2,3,1,0:T(8,128)} fusion(f32[32,8,128,128]{3,2,1,0:T(8,128)} %copy-done.1, f32[32,32]{1,0:T(8,128)S(1)} %copy-done), kind=kOutput, calls=%fused_computation.21 | convolution fusion | flops 1610612736 | bytes 33558528 | tf_op jit(solution)/shard_map/co,oxyz->cxyz/dot_general | solution.py:134
  614.8 21.3 %multiply_bitcast_fusion = f32[1,32,8,128,128]{4,3,2,1,0:T(8,128)} fusion(f32[32,8,128,128]{3,2,1,0:T(8,128)} %get-tuple-element.16, f32[32,8,128,128]{3,2,1,0:T(8,128)} %get-tuple-element.33), kind=kLoop, calls=%fused_computation.28 | loop fusion | flops 8388608 | bytes 50331648 | tf_op jit(solution)/shard_map/broadcast_in_dim | solution.py:137
  671.0 29.0 %fusion.34 = f32[32,8,128,128]{3,2,1,0:T(8,128)} fusion(f32[32,8,16,128]{3,2,1,0:T(8,128)S(1)} %fusion.150, f32[32,8,16,128]{3,2,1,0:T(8,128)S(1)} %fusion.138), kind=kOutput, calls=%fused_computation.63 | convolution fusion | flops 805859328 | bytes 20971520 | tf_op jit(solution)/shard_map/cxky,zk->cxyz/dot_general | solution.py:79
  700.0 45.7 %fusion.1 = f32[1,32,8,128,128]{4,3,2,1,0:T(8,128)} fusion(f32[8,128,128,32]{2,3,1,0:T(8,128)S(1)} %bitcast.320, f32[32,8,128,128]{3,2,1,0:T(8,128)} %fusion.34, f32[32,8,16,128]{3,2,1,0:T(8,128)S(1)} %fusion.136, f32[32,8,16,128]{3,2,1,0:T(8,128)S(1)} %fusion.148), kind=kOutput, calls=%fused_computation.4 | convolution fusion | flops 814247936 | bytes 54525952 | tf_op jit(solution)/shard_map/cxky,zk->cxyz/dot_general | solution.py:79
  745.8 583.1 %all-gather.3.cloned.1.call-done = f32[4,32,32,32,32]{4,3,2,1,0:T(8,128)} async-done(((f32[2,32,32,32,32]{4,3,2,1,0:T(8,128)}), f32[4,32,32,32,32]{4,3,2,1,0:T(8,128)}) %all-gather.3.cloned.1.call-update) | async-done | bytes 16777232 | tf_op jit(solution)/shard_map/all_gather | solution.py:123
  1328.9 34.3 %reduce_sum.9 = f32[2,32,32,32,32]{4,3,2,1,0:T(8,128)} reduce(f32[2,2,32,32,32,32]{5,4,3,2,1,0:T(8,128)} %bitcast.88, f32[]{:T(128)} %constant.27.clone.1), dimensions={0}, to_apply=%region_0.1 | reduce | flops 2097152 | bytes 25165828 | tf_op jit(solution)/shard_map/reduce_sum | solution.py:123
  1363.2 26.1 %reshape.58 = f32[2,32,32,1024]{3,2,1,0:T(8,128)} reshape(f32[2,32,32,32,32]{4,3,2,1,0:T(8,128)} %reduce_sum.9) | data formatting | bytes 16777216 | tf_op jit(solution)/shard_map/reshape | solution.py:124
  (111 shorter events, 183.9 us)
Async XLA Ops:
  7.2 185.6 %copy-start = (f32[32,32]{1,0:T(8,128)S(1)}, f32[32,32]{1,0:T(8,128)}, u32[]{:S(2)}) copy-start(f32[32,32]{1,0:T(8,128)} %param.7) | copy-start | bytes 12292
  7.2 249.1 %copy-start.10 = (s32[32]{0:T(128)}, s32[32]{0:T(128)S(1)}, u32[]{:S(2)}) copy-start(s32[32]{0:T(128)S(1)} %compare_select_fusion) | copy-start | bytes 388
  7.2 17.3 %copy-start.2 = (f32[1,32,8,128,128]{4,3,2,1,0:T(8,128)S(1)}, f32[1,32,8,128,128]{4,3,2,1,0:T(8,128)}, u32[]{:S(2)}) copy-start(f32[1,32,8,128,128]{4,3,2,1,0:T(8,128)} %param.4) | copy-start | bytes 50331652
  90.9 39.3 %all-to-all-start = ((f32[16,1,16384]{2,1,0:T(1,128)}), f32[16,1,16384]{2,1,0:T(1,128)S(1)}, u32[]{:S(2)}, u32[]{:S(2)}) async-start(f32[16,1,16384]{2,1,0:T(1,128)} %reshape.84), calls=%async_computation | async-start | bytes 2097152 | tf_op jit(solution)/shard_map/all_to_all | solution.py:99
  156.5 16.3 %copy-start.5 = (f32[32,32,32]{1,0,2:T(8,128)}, f32[32,32,32]{1,0,2:T(8,128)S(1)}, u32[]{:S(2)}) copy-start(f32[32,32,32]{1,0,2:T(8,128)S(1)} %fusion.76) | copy-start | bytes 393220
  160.1 12.7 copy-start.7
  186.7 36.6 %all-to-all-start.1 = ((f32[16,1,16384]{2,1,0:T(1,128)}), f32[16,1,16384]{2,1,0:T(1,128)S(1)}, u32[]{:S(2)}, u32[]{:S(2)}) async-start(f32[16,1,16384]{2,1,0:T(1,128)} %reshape.86), calls=%async_computation.1 | async-start | bytes 2097152 | tf_op jit(solution)/shard_map/all_to_all | solution.py:108
  192.7 1136.1 %all-gather.3.cloned.1.call-start = ((), (), s32[]{:S(2)}) async-start(), calls=%async_computation.4 | async-start | bytes 100663296 | tf_op jit(solution)/shard_map/all_gather | solution.py:123
  254.3 4.0 copy-start.4
  258.3 29.0 %copy-start.9 = (f32[32,8,16,128]{3,2,1,0:T(8,128)S(1)}, f32[32,8,16,128]{3,2,1,0:T(8,128)}, u32[]{:S(2)}) copy-start(f32[32,8,16,128]{3,2,1,0:T(8,128)} %fusion.142) | copy-start | bytes 6291460
  356.8 14.6 %copy-start.1 = (f32[32,8,128,128]{3,2,1,0:T(8,128)}, f32[32,8,128,128]{3,2,1,0:T(8,128)S(1)}, u32[]{:S(2)}) copy-start(f32[32,8,128,128]{3,2,1,0:T(8,128)S(1)} %get-tuple-element.15) | copy-start | bytes 50331652
  371.4 14.8 %copy-start.11 = (s32[32]{0:T(128)S(1)}, s32[32]{0:T(128)}, u32[]{:S(2)}) copy-start(s32[32]{0:T(128)} %copy-done.10) | copy-start | bytes 388
  490.9 14.1 %copy-start.6 = (f32[32,32,32]{1,0,2:T(8,128)S(1)}, f32[32,32,32]{1,0,2:T(8,128)}, u32[]{:S(2)}) copy-start(f32[32,32,32]{1,0,2:T(8,128)} %copy-done.5) | copy-start | bytes 393220
  490.9 14.1 %copy-start.8 = (f32[32,32,32]{1,0,2:T(8,128)S(1)}, f32[32,32,32]{1,0,2:T(8,128)}, u32[]{:S(2)}) copy-start(f32[32,32,32]{1,0,2:T(8,128)} %copy-done.7) | copy-start | bytes 393220
  609.7 28.0 %all-to-all-start.3 = ((f32[16,1,16384]{2,1,0:T(1,128)}), f32[16,1,16384]{2,1,0:T(1,128)S(1)}, u32[]{:S(2)}, u32[]{:S(2)}) async-start(f32[16,1,16384]{2,1,0:T(1,128)} %reshape.90), calls=%async_computation.3 | async-start | bytes 2097152 | tf_op jit(solution)/shard_map/all_to_all | solution.py:132
  662.9 4.0 copy-start.3
  668.9 31.1 %slice-start = ((s8[16777216]{0:T(1024)(128)(4,1)}), s8[4194304]{0:T(1024)(128)(4,1)S(1)}, s32[]{:S(2)}) async-start(s8[16777216]{0:T(1024)(128)(4,1)} %bitcast.319), calls=%async_computation.5 | async-start | bytes 8388608
  671.0 29.1 %slice-start.1 = ((s8[16777216]{0:T(1024)(128)(4,1)}), s8[4194304]{0:T(1024)(128)(4,1)S(1)}, s32[]{:S(2)}) async-start(s8[16777216]{0:T(1024)(128)(4,1)} %bitcast.319), calls=%async_computation.6 | async-start | bytes 8388608
  671.0 29.1 %slice-start.2 = ((s8[16777216]{0:T(1024)(128)(4,1)}), s8[4194304]{0:T(1024)(128)(4,1)S(1)}, s32[]{:S(2)}) async-start(s8[16777216]{0:T(1024)(128)(4,1)} %bitcast.319), calls=%async_computation.7 | async-start | bytes 8388608
  671.0 29.1 %slice-start.3 = ((s8[16777216]{0:T(1024)(128)(4,1)}), s8[4194304]{0:T(1024)(128)(4,1)S(1)}, s32[]{:S(2)}) async-start(s8[16777216]{0:T(1024)(128)(4,1)} %bitcast.319), calls=%async_computation.8 | async-start | bytes 8388608
Sparse Core Ops, SparseCore 0:
  560.6 768.2 all-gather.2
